TPU v7x, 512 devices: a whole 4x8x8 slice. The times are simulated.
512 devices in a mesh: pipe: 8 (over y), seq: 8 (over x, core), dp: 8 (over z).
Axes of the slice: x: 4, y: 8, z: 8, core: 2. Of those that a mesh axis runs over, the one named last changes fastest.
Arguments:
- incoming: bfloat16 [8, 3, 8, 1024, 1536], P('pipe', None, 'dp', 'seq'), may hold values from -9 to 9, as said below
- contacts: int32 [10, 8, 1024], P(None, 'dp', 'seq'), may hold values from 0 to 15
- keyframes: int32 [10, 8, 1024], P(None, 'dp'), may hold values 0 or 1
- timesteps: int32 [10, 8], P(None, 'dp'), may hold values from 0 to 999
- w_query: bfloat16 [8, 1536, 1536], P('pipe', ('seq', 'dp')), may hold values from -1 to 1, as said below
- w_keyval: bfloat16 [8, 1536, 1536], P('pipe', ('seq', 'dp')), may hold values from -1 to 1, as said below
- norm_gain: float32 [8, 1536], P('pipe'), may hold values from 0.5 to 1.5
- time_freq: float32 [8, 1536], P('pipe'), may hold values from 0.0005 to 0.05
- contact_table: bfloat16 [8, 16, 1536], P('pipe'), may hold values from -3 to 3
- key_bias: float32 [8, 16], P('pipe'), may hold values from 0.5 to 4
- attn_gate: float32 [8, 1536], P('pipe'), may hold values from 1 to 4
- head_cotangent: bfloat16 [8, 3, 8, 1024, 256], P('pipe', None, 'dp', 'seq'), may hold values from -6 to 6
Outputs:
- section_out: bfloat16 [8, 3, 8, 1024, 1536], P('pipe', None, 'dp', 'seq')
- head_grad: float32 [8, 1536, 256], P('pipe', ('seq', 'dp'))
Inputs may be any that keep to these rules, and one draw needn't show every extreme that they name: `contacts`: each frame's contact state, four limbs as bits. `incoming`: activations of order one. `w_query`: entries of about 1536 ** -0.5. `w_keyval`: entries of about 1536 ** -0.5.
All inputs are finite; a program needn't handle non-finite values. No bound on the sum of `keyframes` on one device may be relied on, other than what follows from the above.
Results may differ from a plain program's by a relative error of at most 0.014.
Values may be sent and summed in bfloat16 or wider, within the bound.
A program may use at most 64 MiB of HBM per device.

v0:
```python
import jax
import jax.numpy as jnp
from jax import lax
from jax.sharding import PartitionSpec as P

epsilon = 1e-06


def passed_along(value, axis, steps):
    count = lax.axis_size(axis)
    first, last = (max(0, -steps), min(count, count - steps))
    return lax.ppermute(value, axis, [(source, source + steps) for source in range(first, last)])


def body(
    incoming,
    contacts,
    keyframes,
    timesteps,
    w_query,
    w_keyval,
    norm_gain,
    time_freq,
    contact_table,
    key_bias,
    attn_gate,
    head_cotangent,
):
    section_idx = lax.axis_index("pipe")
    seq_idx = lax.axis_index("seq")
    seq_count = lax.axis_size("seq")
    section_count = lax.axis_size("pipe")
    rep_count = lax.axis_size("dp")
    tok_rows = incoming.shape[3]
    width = incoming.shape[4]
    turns = incoming.shape[1]
    frames = tok_rows * seq_count
    heads_all = key_bias.shape[1]
    head_size = width // heads_all
    heads_local = heads_all // seq_count
    kv_width = w_keyval.shape[2]
    kv_local = kv_width // (2 * head_size * seq_count)
    group_size = heads_local // kv_local
    feat_count = head_cotangent.shape[4]
    score_scale = head_size ** (-0.5)
    gathered = (
        lax.all_gather(w_query, ("seq", "dp"), axis=1, tiled=True),
        lax.all_gather(w_keyval, ("seq", "dp"), axis=1, tiled=True),
    )
    wquery = gathered[0][0]
    wkeyval = gathered[1][0]
    gain_row = norm_gain[0]
    freq_row = time_freq[0]
    table = contact_table[0]
    gate_row = attn_gate[0]
    bias_local = lax.dynamic_slice_in_dim(key_bias[0], seq_idx * heads_local, heads_local)
    contact_all = contacts[:, 0, :]
    key_all = keyframes[:, 0, :]
    step_all = timesteps[:, 0]
    labels = jnp.arange(table.shape[0], dtype=jnp.int32)
    outputs = []
    handed = None
    for turn in range(turns):
        fresh_rows = incoming[0, turn, 0]
        if turn == 0:
            current = fresh_rows
        else:
            current = jnp.where(section_idx == 0, fresh_rows, handed)
        batch_idx = turn - section_idx + section_count - 1
        contact_rows = lax.dynamic_index_in_dim(contact_all, batch_idx, 0, keepdims=False)
        key_flags = lax.dynamic_index_in_dim(key_all, batch_idx, 0, keepdims=False).astype(
            jnp.float32
        )
        timestep = lax.dynamic_index_in_dim(step_all, batch_idx, 0, keepdims=False).astype(
            jnp.float32
        )
        onehot = (contact_rows[:, None] == labels[None, :]).astype(jnp.bfloat16)
        embedded = jnp.dot(onehot, table, preferred_element_type=jnp.float32)
        hidden = current.astype(jnp.float32) + embedded
        root_mean = jnp.sqrt(jnp.mean(hidden * hidden, axis=-1, keepdims=True) + epsilon)
        modulation = gain_row * (1.0 + 0.5 * jnp.sin(timestep * freq_row))
        normed = (hidden / root_mean * modulation[None, :]).astype(jnp.bfloat16)
        queries = jnp.dot(normed, wquery, preferred_element_type=jnp.float32).astype(jnp.bfloat16)
        keyval = jnp.dot(normed, wkeyval, preferred_element_type=jnp.float32).astype(jnp.bfloat16)
        query_parts = queries.reshape(tok_rows, seq_count, width // seq_count)
        keyval_parts = keyval.reshape(tok_rows, seq_count, kv_width // seq_count)
        regrouped = (
            lax.all_to_all(query_parts, "seq", split_axis=1, concat_axis=0, tiled=True),
            lax.all_to_all(keyval_parts, "seq", split_axis=1, concat_axis=0, tiled=True),
        )
        query_heads = regrouped[0].reshape(frames, heads_local, head_size)
        keyval_heads = regrouped[1].reshape(frames, kv_local, 2, head_size)
        head_outputs = []
        for head in range(heads_local):
            key_rows = keyval_heads[:, head // group_size, 0]
            value_rows = keyval_heads[:, head // group_size, 1]
            scores = (
                lax.dot_general(
                    query_heads[:, head],
                    key_rows,
                    (((1,), (1,)), ((), ())),
                    preferred_element_type=jnp.float32,
                )
                * score_scale
            )
            scores = scores + bias_local[head] * key_flags[None, :]
            row_max = jnp.max(scores, axis=-1, keepdims=True)
            exponent = jnp.exp(scores - row_max)
            probabilities = (exponent / jnp.sum(exponent, axis=-1, keepdims=True)).astype(
                jnp.bfloat16
            )
            head_outputs.append(
                jnp.dot(probabilities, value_rows, preferred_element_type=jnp.float32).astype(
                    jnp.bfloat16
                )
            )
        attended = jnp.stack(head_outputs, axis=1).reshape(frames, heads_local * head_size)
        returned = lax.all_to_all(attended, "seq", split_axis=0, concat_axis=1, tiled=True)
        output = (hidden + gate_row[None, :] * returned.astype(jnp.float32)).astype(jnp.bfloat16)
        outputs.append(output)
        if turn + 1 < turns:
            handed = passed_along(output, "pipe", 1)
    stacked = jnp.stack(outputs)
    section_out = stacked[None, :, None]
    flat_out = stacked.reshape(turns * tok_rows, width)
    flat_cot = head_cotangent[0, :, 0].reshape(turns * tok_rows, feat_count)
    factor = float(turns * rep_count * frames) ** (-0.5)
    grad_rows = lax.psum_scatter(
        lax.dot_general(
            flat_out, flat_cot, (((0,), (0,)), ((), ())), preferred_element_type=jnp.float32
        )
        * factor,
        ("seq", "dp"),
        scatter_dimension=0,
        tiled=True,
    )
    return (section_out, grad_rows[None])


def solution(mesh):
    in_specs = (
        P("pipe", None, "dp", "seq", None),
        P(None, "dp", "seq"),
        P(None, "dp", None),
        P(None, "dp"),
        P("pipe", ("seq", "dp"), None),
        P("pipe", ("seq", "dp"), None),
        P("pipe", None),
        P("pipe", None),
        P("pipe", None, None),
        P("pipe", None),
        P("pipe", None),
        P("pipe", None, "dp", "seq", None),
    )
    out_specs = (P("pipe", None, "dp", "seq", None), P("pipe", ("seq", "dp"), None))
    return jax.shard_map(body, mesh=mesh, in_specs=in_specs, out_specs=out_specs, check_vma=False)
```

profile of v0, /device:TPU:8, one launch (start us, length us, event | category | flops | bytes accessed | tf_op | source)
XLA Modules:
  0.0 502.9 jit_solution(17415926230523855256)
XLA Ops:
  15.4 86.2 %all-gather.3.cloned.1.call-done = bf16[1,1536,1536]{2,1,0:T(8,128)(2,1)} async-done(((bf16[1,24,1536]{2,1,0:T(8,128)(2,1)}), bf16[1,1536,1536]{2,1,0:T(8,128)(2,1)}) %all-gather.3.cloned.1.call-update) | async-done | bytes 4718608 | tf_op jit(solution)/shard_map/all_gather | solution.py:47
  105.7 3.5 all-to-all-start
  109.1 78.3 %all-gather.5.cloned.1.call-done = bf16[1,1536,1536]{2,1,0:T(8,128)(2,1)} async-done(((bf16[1,24,1536]{2,1,0:T(8,128)(2,1)}), bf16[1,1536,1536]{2,1,0:T(8,128)(2,1)}) %all-gather.5.cloned.1.call-update) | async-done | bytes 4718608 | tf_op jit(solution)/shard_map/all_gather | solution.py:48
  191.6 3.5 all-to-all-start.1
  198.2 5.7 %all-to-all-done.1 = bf16[128,8,192]{0,2,1:T(8,128)(2,1)S(1)} async-done(((bf16[128,8,192]{0,2,1:T(8,128)(2,1)}), bf16[128,8,192]{0,2,1:T(8,128)(2,1)S(1)}, u32[]{:S(2)}, u32[]{:S(2)}) %all-to-all-start.1) | async-done | bytes 393248 | tf_op jit(solution)/shard_map/all_to_all | solution.py:89
  211.1 3.5 all-to-all-start.2
  214.6 8.8 %all-to-all-done.2 = bf16[8,128,192]{1,2,0:T(8,128)(2,1)S(1)} async-done(((bf16[8,128,192]{1,2,0:T(8,128)(2,1)}), bf16[8,128,192]{1,2,0:T(8,128)(2,1)S(1)}, u32[]{:S(2)}, u32[]{:S(2)}) %all-to-all-start.2) | async-done | bytes 393248 | tf_op jit(solution)/shard_map/all_to_all | solution.py:118
  223.8 3.4 collective-permute-start
  227.2 9.1 %collective-permute-done = bf16[128,1536]{1,0:T(8,128)(2,1)S(1)} collective-permute-done((bf16[128,1536]{1,0:T(8,128)(2,1)S(1)}, bf16[128,1536]{1,0:T(8,128)(2,1)S(1)}, u32[]{:S(2)}, u32[]{:S(2)}) %collective-permute-start) | collective-permute-done | bytes 393248 | tf_op jit(solution)/shard_map/ppermute | solution.py:12
  237.8 3.2 fusion.27
  241.9 3.6 all-to-all-start.3
  249.6 4.6 all-to-all-done.3
  254.2 3.5 all-to-all-start.4
  258.1 8.4 %all-to-all-done.4 = bf16[128,8,192]{0,2,1:T(8,128)(2,1)S(1)} async-done(((bf16[128,8,192]{0,2,1:T(8,128)(2,1)}), bf16[128,8,192]{0,2,1:T(8,128)(2,1)S(1)}, u32[]{:S(2)}, u32[]{:S(2)}) %all-to-all-start.4) | async-done | bytes 393248 | tf_op jit(solution)/shard_map/all_to_all | solution.py:89
  272.9 11.3 %all_to_all.129 = bf16[8,128,192]{1,2,0:T(8,128)(2,1)S(1)} all-to-all(bf16[8,128,192]{1,2,0:T(8,128)(2,1)S(1)} %copy.47), channel_id=1, replica_groups=mesh['pipe'=8,'seq'=8,'dp'=8] {'seq'}, dimensions={0} | all-to-all | bytes 786432 | tf_op jit(solution)/shard_map/all_to_all | solution.py:118
  284.7 3.4 collective-permute-start.1
  288.4 8.8 %collective-permute-done.1 = bf16[128,1536]{1,0:T(8,128)(2,1)S(1)} collective-permute-done((bf16[128,1536]{1,0:T(8,128)(2,1)S(1)}, bf16[128,1536]{1,0:T(8,128)(2,1)S(1)}, u32[]{:S(2)}, u32[]{:S(2)}) %collective-permute-start.1) | collective-permute-done | bytes 393248 | tf_op jit(solution)/shard_map/ppermute | solution.py:12
  298.5 3.2 fusion.30
  302.6 3.5 all-to-all-start.6
  310.2 4.8 all-to-all-done.6
  314.9 3.5 all-to-all-start.7
  319.1 8.1 %all-to-all-done.7 = bf16[128,8,192]{0,2,1:T(8,128)(2,1)S(1)} async-done(((bf16[128,8,192]{0,2,1:T(8,128)(2,1)}), bf16[128,8,192]{0,2,1:T(8,128)(2,1)S(1)}, u32[]{:S(2)}, u32[]{:S(2)}) %all-to-all-start.7) | async-done | bytes 393248 | tf_op jit(solution)/shard_map/all_to_all | solution.py:89
  333.6 11.3 %all_to_all.130 = bf16[8,128,192]{1,2,0:T(8,128)(2,1)S(1)} all-to-all(bf16[8,128,192]{1,2,0:T(8,128)(2,1)S(1)} %copy.53), channel_id=1, replica_groups=mesh['pipe'=8,'seq'=8,'dp'=8] {'seq'}, dimensions={0} | all-to-all | bytes 786432 | tf_op jit(solution)/shard_map/all_to_all | solution.py:118
  348.3 148.0 %reduce-scatter.4.cloned.1.call-done = f32[24,256]{1,0:T(8,128)} async-done(((f32[1536,256]{1,0:T(8,128)}), f32[24,256]{1,0:T(8,128)}) %reduce-scatter.4.cloned.1.call-update) | async-done | bytes 24592
  (89 shorter events, 55.6 us)
Async XLA Ops:
  7.2 339.4 %copy-start = (bf16[1,3,1,128,256]{4,3,2,1,0:T(8,128)(2,1)S(1)}, bf16[1,3,1,128,256]{4,3,2,1,0:T(8,128)(2,1)}, u32[]{:S(2)}) copy-start(bf16[1,3,1,128,256]{4,3,2,1,0:T(8,128)(2,1)} %param.23) | copy-start | bytes 589828
  7.2 94.4 %all-gather.3.cloned.1.call-start = ((), (), s32[]{:S(2)}) async-start(), calls=%async_computation.10 | async-start | bytes 4792320 | tf_op jit(solution)/shard_map/all_gather | solution.py:47
  7.9 179.6 %all-gather.5.cloned.1.call-start = ((), (), s32[]{:S(2)}) async-start(), calls=%async_computation.11 | async-start | bytes 4792320 | tf_op jit(solution)/shard_map/all_gather | solution.py:48
  105.7 85.9 %all-to-all-start = ((bf16[128,8,192]{0,2,1:T(8,128)(2,1)}), bf16[128,8,192]{0,2,1:T(8,128)(2,1)S(1)}, u32[]{:S(2)}, u32[]{:S(2)}) async-start(bf16[128,8,192]{0,2,1:T(8,128)(2,1)} %bitcast.5), calls=%async_computation | async-start | bytes 786432 | tf_op jit(solution)/shard_map/all_to_all | solution.py:88
  109.1 85.9 %copy-start.3 = (f32[1,16]{1,0:T(1,128)S(1)}, f32[1,16]{1,0:T(1,128)}, u32[]{:S(2)}) copy-start(f32[1,16]{1,0:T(1,128)} %param.21) | copy-start | bytes 196
  191.6 12.3 %all-to-all-start.1 = ((bf16[128,8,192]{0,2,1:T(8,128)(2,1)}), bf16[128,8,192]{0,2,1:T(8,128)(2,1)S(1)}, u32[]{:S(2)}, u32[]{:S(2)}) async-start(bf16[128,8,192]{0,2,1:T(8,128)(2,1)} %bitcast.10), calls=%async_computation.1 | async-start | bytes 786432 | tf_op jit(solution)/shard_map/all_to_all | solution.py:89
  208.9 5.6 %copy-start.2 = (f32[1,1536]{1,0:T(1,128)S(1)}, f32[1,1536]{1,0:T(1,128)}, u32[]{:S(2)}) copy-start(f32[1,1536]{1,0:T(1,128)} %param.22) | copy-start | bytes 18436
  210.1 26.3 %copy-start.1 = (bf16[1,16,1536]{2,1,0:T(8,128)(2,1)S(1)}, bf16[1,16,1536]{2,1,0:T(8,128)(2,1)}, u32[]{:S(2)}) copy-start(bf16[1,16,1536]{2,1,0:T(8,128)(2,1)} %param.20) | copy-start | bytes 147460
  211.1 12.3 %all-to-all-start.2 = ((bf16[8,128,192]{1,2,0:T(8,128)(2,1)}), bf16[8,128,192]{1,2,0:T(8,128)(2,1)S(1)}, u32[]{:S(2)}, u32[]{:S(2)}) async-start(bf16[8,128,192]{1,2,0:T(8,128)(2,1)} %copy.41), calls=%async_computation.2 | async-start | bytes 786432 | tf_op jit(solution)/shard_map/all_to_all | solution.py:118
  223.8 12.6 %collective-permute-start = (bf16[128,1536]{1,0:T(8,128)(2,1)S(1)}, bf16[128,1536]{1,0:T(8,128)(2,1)S(1)}, u32[]{:S(2)}, u32[]{:S(2)}) collective-permute-start(bf16[128,1536]{1,0:T(8,128)(2,1)S(1)} %add_convert_fusion.2), channel_id=1, source_target_pairs={{0,64},{64,128},{128,192},{192,256},{256,320},{320,384},{384,448},... | collective-permute-start | bytes 1179656 | tf_op jit(solution)/shard_map/ppermute | solution.py:12
  241.9 12.3 %all-to-all-start.3 = ((bf16[128,8,192]{0,2,1:T(8,128)(2,1)}), bf16[128,8,192]{0,2,1:T(8,128)(2,1)S(1)}, u32[]{:S(2)}, u32[]{:S(2)}) async-start(bf16[128,8,192]{0,2,1:T(8,128)(2,1)} %bitcast.28), calls=%async_computation.3 | async-start | bytes 786432 | tf_op jit(solution)/shard_map/all_to_all | solution.py:88
  254.2 12.3 %all-to-all-start.4 = ((bf16[128,8,192]{0,2,1:T(8,128)(2,1)}), bf16[128,8,192]{0,2,1:T(8,128)(2,1)S(1)}, u32[]{:S(2)}, u32[]{:S(2)}) async-start(bf16[128,8,192]{0,2,1:T(8,128)(2,1)} %bitcast.32), calls=%async_computation.4 | async-start | bytes 786432 | tf_op jit(solution)/shard_map/all_to_all | solution.py:89
  284.7 12.6 %collective-permute-start.1 = (bf16[128,1536]{1,0:T(8,128)(2,1)S(1)}, bf16[128,1536]{1,0:T(8,128)(2,1)S(1)}, u32[]{:S(2)}, u32[]{:S(2)}) collective-permute-start(bf16[128,1536]{1,0:T(8,128)(2,1)S(1)} %add_convert_fusion.1), channel_id=1, source_target_pairs={{0,64},{64,128},{128,192},{192,256},{256,320},{320,384},{384,448},... | collective-permute-start | bytes 1179656 | tf_op jit(solution)/shard_map/ppermute | solution.py:12
  302.6 12.3 %all-to-all-start.6 = ((bf16[128,8,192]{0,2,1:T(8,128)(2,1)}), bf16[128,8,192]{0,2,1:T(8,128)(2,1)S(1)}, u32[]{:S(2)}, u32[]{:S(2)}) async-start(bf16[128,8,192]{0,2,1:T(8,128)(2,1)} %bitcast.48), calls=%async_computation.6 | async-start | bytes 786432 | tf_op jit(solution)/shard_map/all_to_all | solution.py:88
  314.9 12.3 %all-to-all-start.7 = ((bf16[128,8,192]{0,2,1:T(8,128)(2,1)}), bf16[128,8,192]{0,2,1:T(8,128)(2,1)S(1)}, u32[]{:S(2)}, u32[]{:S(2)}) async-start(bf16[128,8,192]{0,2,1:T(8,128)(2,1)} %bitcast.52), calls=%async_computation.7 | async-start | bytes 786432 | tf_op jit(solution)/shard_map/all_to_all | solution.py:89
  318.4 177.9 %reduce-scatter.4.cloned.1.call-start = ((), (), s32[]{:S(2)}) async-start(), calls=%async_computation.12 | async-start | bytes 1597440
Sparse Core Ops, SparseCore 0:
  11.3 90.1 all-gather.2
  104.9 82.5 all-gather.4
  348.5 147.8 reduce-scatter.3
where the time goes:
time: 504 us; the launch traced here: 503 us
  waiting for transfers between devices  372 us (74%)
  matrix products  35.7 us (7%)
  starting transfers between devices  31.5 us (6%)
  blocking collectives  22.7 us (5%)
  between operations  16.2 us (3%)
  local copies, waits for them, and re-layouts  12.8 us (3%)
  other arithmetic  11.6 us (2%)
    unnamed x4, waiting for transfers between devices  149 us
    all_gather x1, waiting for transfers between devices, body(): lax.all_gather(w_query, ('seq', 'dp'), axis=1, tiled=True)  86.2 us
    all_gather x1, waiting for transfers between devices, body(): lax.all_gather(w_keyval, ('seq', 'dp'), axis=1, tiled=True)  78.3 us
    all_to_all x2, blocking collectives, body(): lax.all_to_all(attended, 'seq', split_axis=0, concat_axis=1, tiled=True)  22.7 us
    all_to_all x3, waiting for transfers between devices, body(): lax.all_to_all(keyval_parts, 'seq', split_axis=1, concat_axis=0, tiled=True)  22.2 us
    ppermute x2, waiting for transfers between devices, passed_along(): lax.ppermute(value, axis, [(source, source + steps) for source in range(f...  18 us
    all_to_all x3, starting transfers between devices, body(): lax.all_to_all(query_parts, 'seq', split_axis=1, concat_axis=0, tiled=True)  10.5 us
    all_to_all x3, starting transfers between devices, body(): lax.all_to_all(keyval_parts, 'seq', split_axis=1, concat_axis=0, tiled=True)  10.4 us
  transfers between devices with their start and end apart: 12, of which 11 were waited for; matrix products, arithmetic and copies ran while one was open for 5% of the time, Pallas kernels for 0%

commit v1 on v0

--- a/solution.py
+++ b/solution.py
@@ -44,7 +44,12 @@
     feat_count = head_cotangent.shape[4]
     score_scale = head_size ** (-0.5)
     gathered = (
-        lax.all_gather(w_query, ("seq", "dp"), axis=1, tiled=True),
+        jnp.concatenate(
+            lax.all_to_all(
+                jnp.stack([w_query] * lax.axis_size(("seq", "dp"))), ("seq", "dp"), 0, 0
+            ),
+            axis=1,
+        ),
         lax.all_gather(w_keyval, ("seq", "dp"), axis=1, tiled=True),
     )
     wquery = gathered[0][0]

time: 504 us -> 475 us (0.942)
  waiting for transfers between devices: 372 us -> 326 us
  starting transfers between devices: 31.5 us -> 46 us
    all_to_all x0 -> x1, waiting for transfers between devices: none -> 113 us  [body(): lax.all_to_all(jnp.stack([w_query] * lax.axis_size(('seq', 'dp'))), ('seq...]
    all_gather x1 -> x0, waiting for transfers between devices: 86.2 us -> none  [body(): lax.all_gather(w_query, ('seq', 'dp'), axis=1, tiled=True)]
    all_gather x1, waiting for transfers between devices: 78.3 us -> 0.02 us  [body(): lax.all_gather(w_keyval, ('seq', 'dp'), axis=1, tiled=True)]
    all_to_all x0 -> x1, starting transfers between devices: none -> 14.2 us  [body(): lax.all_to_all(jnp.stack([w_query] * lax.axis_size(('seq', 'dp'))), ('seq...]
    unnamed x4 -> x3, waiting for transfers between devices: 149 us -> 150 us
where the time goes in v1:
time: 475 us; the launch traced here: 474 us
  waiting for transfers between devices  326 us (69%)
  starting transfers between devices  46 us (10%)
  matrix products  35.9 us (8%)
  blocking collectives  22.7 us (5%)
  between operations  16.5 us (3%)
  local copies, waits for them, and re-layouts  15.5 us (3%)
  other arithmetic  10.9 us (2%)
    unnamed x3, waiting for transfers between devices  150 us
    all_to_all x1, waiting for transfers between devices, body(): lax.all_to_all(jnp.stack([w_query] * lax.axis_size(('seq', 'dp'))), ('seq...  113 us
    all_to_all x2, blocking collectives, body(): lax.all_to_all(attended, 'seq', split_axis=0, concat_axis=1, tiled=True)  22.7 us
    all_to_all x3, waiting for transfers between devices, body(): lax.all_to_all(keyval_parts, 'seq', split_axis=1, concat_axis=0, tiled=True)  22.2 us
    ppermute x2, waiting for transfers between devices, passed_along(): lax.ppermute(value, axis, [(source, source + steps) for source in range(f...  17.6 us
    all_to_all x3, waiting for transfers between devices, body(): lax.all_to_all(query_parts, 'seq', split_axis=1, concat_axis=0, tiled=True)  14.3 us
    all_to_all x1, starting transfers between devices, body(): lax.all_to_all(jnp.stack([w_query] * lax.axis_size(('seq', 'dp'))), ('seq...  14.2 us
    all_to_all x3, starting transfers between devices, body(): lax.all_to_all(query_parts, 'seq', split_axis=1, concat_axis=0, tiled=True)  10.6 us
  transfers between devices with their start and end apart: 12, of which 11 were waited for; matrix products, arithmetic and copies ran while one was open for 5% of the time, Pallas kernels for 0%

profile of v1, /device:TPU:8, one launch (start us, length us, event | category | flops | bytes accessed | tf_op | source)
XLA Modules:
  0.0 473.8 jit_solution(14011235986251828745)
XLA Ops:
  7.2 3.5 stack.28
  10.7 14.2 %all-to-all-start = ((bf16[64,1,24,1536]{3,2,1,0:T(8,128)(2,1)}), bf16[64,1,24,1536]{3,2,1,0:T(8,128)(2,1)}, u32[]{:S(2)}, u32[]{:S(2)}) async-start(bf16[64,1,24,1536]{3,2,1,0:T(8,128)(2,1)} %stack.28), calls=%async_computation | async-start | bytes 9437184 | tf_op jit(solution)/shard_map/all_to_all | solution.py:48
  30.8 113.2 %all-to-all-done = bf16[64,1,24,1536]{3,2,1,0:T(8,128)(2,1)} async-done(((bf16[64,1,24,1536]{3,2,1,0:T(8,128)(2,1)}), bf16[64,1,24,1536]{3,2,1,0:T(8,128)(2,1)}, u32[]{:S(2)}, u32[]{:S(2)}) %all-to-all-start) | async-done | bytes 4718624 | tf_op jit(solution)/shard_map/all_to_all | solution.py:48
  148.1 3.7 all-to-all-start.1
  155.9 4.8 %all-to-all-done.1 = bf16[128,8,192]{0,2,1:T(8,128)(2,1)S(1)} async-done(((bf16[128,8,192]{0,2,1:T(8,128)(2,1)}), bf16[128,8,192]{0,2,1:T(8,128)(2,1)S(1)}, u32[]{:S(2)}, u32[]{:S(2)}) %all-to-all-start.1) | async-done | bytes 393248 | tf_op jit(solution)/shard_map/all_to_all | solution.py:93
  160.7 3.5 all-to-all-start.2
  167.4 5.7 %all-to-all-done.2 = bf16[128,8,192]{0,2,1:T(8,128)(2,1)S(1)} async-done(((bf16[128,8,192]{0,2,1:T(8,128)(2,1)}), bf16[128,8,192]{0,2,1:T(8,128)(2,1)S(1)}, u32[]{:S(2)}, u32[]{:S(2)}) %all-to-all-start.2) | async-done | bytes 393248 | tf_op jit(solution)/shard_map/all_to_all | solution.py:94
  180.2 3.5 all-to-all-start.3
  183.7 8.8 %all-to-all-done.3 = bf16[8,128,192]{1,2,0:T(8,128)(2,1)S(1)} async-done(((bf16[8,128,192]{1,2,0:T(8,128)(2,1)}), bf16[8,128,192]{1,2,0:T(8,128)(2,1)S(1)}, u32[]{:S(2)}, u32[]{:S(2)}) %all-to-all-start.3) | async-done | bytes 393248 | tf_op jit(solution)/shard_map/all_to_all | solution.py:123
  193.0 3.7 collective-permute-start
  196.6 8.9 %collective-permute-done = bf16[128,1536]{1,0:T(8,128)(2,1)S(1)} collective-permute-done((bf16[128,1536]{1,0:T(8,128)(2,1)S(1)}, bf16[128,1536]{1,0:T(8,128)(2,1)S(1)}, u32[]{:S(2)}, u32[]{:S(2)}) %collective-permute-start) | collective-permute-done | bytes 393248 | tf_op jit(solution)/shard_map/ppermute | solution.py:12
  211.0 3.5 all-to-all-start.4
  218.6 4.7 all-to-all-done.4
  223.4 3.5 all-to-all-start.5
  227.3 8.4 %all-to-all-done.5 = bf16[128,8,192]{0,2,1:T(8,128)(2,1)S(1)} async-done(((bf16[128,8,192]{0,2,1:T(8,128)(2,1)}), bf16[128,8,192]{0,2,1:T(8,128)(2,1)S(1)}, u32[]{:S(2)}, u32[]{:S(2)}) %all-to-all-start.5) | async-done | bytes 393248 | tf_op jit(solution)/shard_map/all_to_all | solution.py:94
  242.1 11.3 %all_to_all.134 = bf16[8,128,192]{1,2,0:T(8,128)(2,1)S(1)} all-to-all(bf16[8,128,192]{1,2,0:T(8,128)(2,1)S(1)} %copy.47), channel_id=1, replica_groups=mesh['pipe'=8,'seq'=8,'dp'=8] {'seq'}, dimensions={0} | all-to-all | bytes 786432 | tf_op jit(solution)/shard_map/all_to_all | solution.py:123
  253.9 3.5 collective-permute-start.1
  257.7 8.8 %collective-permute-done.1 = bf16[128,1536]{1,0:T(8,128)(2,1)S(1)} collective-permute-done((bf16[128,1536]{1,0:T(8,128)(2,1)S(1)}, bf16[128,1536]{1,0:T(8,128)(2,1)S(1)}, u32[]{:S(2)}, u32[]{:S(2)}) %collective-permute-start.1) | collective-permute-done | bytes 393248 | tf_op jit(solution)/shard_map/ppermute | solution.py:12
  271.8 3.5 all-to-all-start.7
  279.4 4.7 %all-to-all-done.7 = bf16[128,8,192]{0,2,1:T(8,128)(2,1)S(1)} async-done(((bf16[128,8,192]{0,2,1:T(8,128)(2,1)}), bf16[128,8,192]{0,2,1:T(8,128)(2,1)S(1)}, u32[]{:S(2)}, u32[]{:S(2)}) %all-to-all-start.7) | async-done | bytes 393248 | tf_op jit(solution)/shard_map/all_to_all | solution.py:93
  284.1 3.5 all-to-all-start.8
  288.3 8.1 %all-to-all-done.8 = bf16[128,8,192]{0,2,1:T(8,128)(2,1)S(1)} async-done(((bf16[128,8,192]{0,2,1:T(8,128)(2,1)}), bf16[128,8,192]{0,2,1:T(8,128)(2,1)S(1)}, u32[]{:S(2)}, u32[]{:S(2)}) %all-to-all-start.8) | async-done | bytes 393248 | tf_op jit(solution)/shard_map/all_to_all | solution.py:94
  302.9 11.3 %all_to_all.135 = bf16[8,128,192]{1,2,0:T(8,128)(2,1)S(1)} all-to-all(bf16[8,128,192]{1,2,0:T(8,128)(2,1)S(1)} %copy.53), channel_id=1, replica_groups=mesh['pipe'=8,'seq'=8,'dp'=8] {'seq'}, dimensions={0} | all-to-all | bytes 786432 | tf_op jit(solution)/shard_map/all_to_all | solution.py:123
  317.6 149.3 %reduce-scatter.4.cloned.1.call-done = f32[24,256]{1,0:T(8,128)} async-done(((f32[1536,256]{1,0:T(8,128)}), f32[24,256]{1,0:T(8,128)}) %reduce-scatter.4.cloned.1.call-update) | async-done | bytes 24592
  (95 shorter events, 59.9 us)
Async XLA Ops:
  7.2 308.7 %copy-start = (bf16[1,3,1,128,256]{4,3,2,1,0:T(8,128)(2,1)S(1)}, bf16[1,3,1,128,256]{4,3,2,1,0:T(8,128)(2,1)}, u32[]{:S(2)}) copy-start(bf16[1,3,1,128,256]{4,3,2,1,0:T(8,128)(2,1)} %param.23) | copy-start | bytes 589828
  10.6 14.9 %copy-start.5 = (s32[10,1]{0,1:T(1,128)S(1)}, s32[10,1]{0,1:T(1,128)}, u32[]{:S(2)}) copy-start(s32[10,1]{0,1:T(1,128)} %param.15) | copy-start | bytes 124
  10.6 18.2 %copy-start.2 = (f32[1,1536]{1,0:T(1,128)S(1)}, f32[1,1536]{1,0:T(1,128)}, u32[]{:S(2)}) copy-start(f32[1,1536]{1,0:T(1,128)} %param.18) | copy-start | bytes 18436
  10.6 18.2 %copy-start.3 = (f32[1,1536]{1,0:T(1,128)S(1)}, f32[1,1536]{1,0:T(1,128)}, u32[]{:S(2)}) copy-start(f32[1,1536]{1,0:T(1,128)} %param.19) | copy-start | bytes 18436
  10.6 18.7 %copy-start.1 = (bf16[1,16,1536]{2,1,0:T(8,128)(2,1)S(1)}, bf16[1,16,1536]{2,1,0:T(8,128)(2,1)}, u32[]{:S(2)}) copy-start(bf16[1,16,1536]{2,1,0:T(8,128)(2,1)} %param.20) | copy-start | bytes 147460
  10.7 133.4 %all-to-all-start = ((bf16[64,1,24,1536]{3,2,1,0:T(8,128)(2,1)}), bf16[64,1,24,1536]{3,2,1,0:T(8,128)(2,1)}, u32[]{:S(2)}, u32[]{:S(2)}) async-start(bf16[64,1,24,1536]{3,2,1,0:T(8,128)(2,1)} %stack.28), calls=%async_computation | async-start | bytes 9437184 | tf_op jit(solution)/shard_map/all_to_all | solution.py:48
  24.8 127.0 %all-gather.2.cloned.1.call-start = ((), (), s32[]{:S(2)}) async-start(), calls=%async_computation.11 | async-start | bytes 4792320 | tf_op jit(solution)/shard_map/all_gather | solution.py:53
  148.1 12.6 %all-to-all-start.1 = ((bf16[128,8,192]{0,2,1:T(8,128)(2,1)}), bf16[128,8,192]{0,2,1:T(8,128)(2,1)S(1)}, u32[]{:S(2)}, u32[]{:S(2)}) async-start(bf16[128,8,192]{0,2,1:T(8,128)(2,1)} %bitcast.6), calls=%async_computation.1 | async-start | bytes 786432 | tf_op jit(solution)/shard_map/all_to_all | solution.py:93
  151.8 12.4 %copy-start.6 = (f32[1,16]{1,0:T(1,128)S(1)}, f32[1,16]{1,0:T(1,128)}, u32[]{:S(2)}) copy-start(f32[1,16]{1,0:T(1,128)} %param.21) | copy-start | bytes 196
  160.7 12.3 %all-to-all-start.2 = ((bf16[128,8,192]{0,2,1:T(8,128)(2,1)}), bf16[128,8,192]{0,2,1:T(8,128)(2,1)S(1)}, u32[]{:S(2)}, u32[]{:S(2)}) async-start(bf16[128,8,192]{0,2,1:T(8,128)(2,1)} %bitcast.11), calls=%async_computation.2 | async-start | bytes 786432 | tf_op jit(solution)/shard_map/all_to_all | solution.py:94
  178.1 5.6 %copy-start.4 = (f32[1,1536]{1,0:T(1,128)S(1)}, f32[1,1536]{1,0:T(1,128)}, u32[]{:S(2)}) copy-start(f32[1,1536]{1,0:T(1,128)} %param.22) | copy-start | bytes 18436
  180.2 12.3 %all-to-all-start.3 = ((bf16[8,128,192]{1,2,0:T(8,128)(2,1)}), bf16[8,128,192]{1,2,0:T(8,128)(2,1)S(1)}, u32[]{:S(2)}, u32[]{:S(2)}) async-start(bf16[8,128,192]{1,2,0:T(8,128)(2,1)} %copy.41), calls=%async_computation.3 | async-start | bytes 786432 | tf_op jit(solution)/shard_map/all_to_all | solution.py:123
  193.0 12.6 %collective-permute-start = (bf16[128,1536]{1,0:T(8,128)(2,1)S(1)}, bf16[128,1536]{1,0:T(8,128)(2,1)S(1)}, u32[]{:S(2)}, u32[]{:S(2)}) collective-permute-start(bf16[128,1536]{1,0:T(8,128)(2,1)S(1)} %add_convert_fusion.2), channel_id=1, source_target_pairs={{0,64},{64,128},{128,192},{192,256},{256,320},{320,384},{384,448},... | collective-permute-start | bytes 1179656 | tf_op jit(solution)/shard_map/ppermute | solution.py:12
  211.0 12.3 %all-to-all-start.4 = ((bf16[128,8,192]{0,2,1:T(8,128)(2,1)}), bf16[128,8,192]{0,2,1:T(8,128)(2,1)S(1)}, u32[]{:S(2)}, u32[]{:S(2)}) async-start(bf16[128,8,192]{0,2,1:T(8,128)(2,1)} %bitcast.29), calls=%async_computation.4 | async-start | bytes 786432 | tf_op jit(solution)/shard_map/all_to_all | solution.py:93
  223.4 12.3 %all-to-all-start.5 = ((bf16[128,8,192]{0,2,1:T(8,128)(2,1)}), bf16[128,8,192]{0,2,1:T(8,128)(2,1)S(1)}, u32[]{:S(2)}, u32[]{:S(2)}) async-start(bf16[128,8,192]{0,2,1:T(8,128)(2,1)} %bitcast.33), calls=%async_computation.5 | async-start | bytes 786432 | tf_op jit(solution)/shard_map/all_to_all | solution.py:94
  253.9 12.6 %collective-permute-start.1 = (bf16[128,1536]{1,0:T(8,128)(2,1)S(1)}, bf16[128,1536]{1,0:T(8,128)(2,1)S(1)}, u32[]{:S(2)}, u32[]{:S(2)}) collective-permute-start(bf16[128,1536]{1,0:T(8,128)(2,1)S(1)} %add_convert_fusion.1), channel_id=1, source_target_pairs={{0,64},{64,128},{128,192},{192,256},{256,320},{320,384},{384,448},... | collective-permute-start | bytes 1179656 | tf_op jit(solution)/shard_map/ppermute | solution.py:12
  271.8 12.3 %all-to-all-start.7 = ((bf16[128,8,192]{0,2,1:T(8,128)(2,1)}), bf16[128,8,192]{0,2,1:T(8,128)(2,1)S(1)}, u32[]{:S(2)}, u32[]{:S(2)}) async-start(bf16[128,8,192]{0,2,1:T(8,128)(2,1)} %bitcast.49), calls=%async_computation.7 | async-start | bytes 786432 | tf_op jit(solution)/shard_map/all_to_all | solution.py:93
  284.1 12.3 %all-to-all-start.8 = ((bf16[128,8,192]{0,2,1:T(8,128)(2,1)}), bf16[128,8,192]{0,2,1:T(8,128)(2,1)S(1)}, u32[]{:S(2)}, u32[]{:S(2)}) async-start(bf16[128,8,192]{0,2,1:T(8,128)(2,1)} %bitcast.53), calls=%async_computation.8 | async-start | bytes 786432 | tf_op jit(solution)/shard_map/all_to_all | solution.py:94
  287.6 179.4 %reduce-scatter.4.cloned.1.call-start = ((), (), s32[]{:S(2)}) async-start(), calls=%async_computation.12 | async-start | bytes 1597440
Sparse Core Ops, SparseCore 0:
  29.0 114.6 all-gather.1
  317.7 149.1 reduce-scatter.3
